TPU v7x, 256 devices: a whole 4x4x8 slice. The times are simulated.
256 devices in a mesh: seq: 128 (over y, x_lo, z, core), tp: 2 (over x_hi).
Axes of the slice: x: 4 (x_hi: 2, x_lo: 2; x = x_hi * 2 + x_lo), y: 4, z: 8, core: 2. Of those that a mesh axis runs over, the one named last changes fastest.
Arguments:
- activations: bfloat16 [32768, 8192], P('seq', 'tp'), may hold values from -400 to 400
- norm_gain: float32 [8192], P('tp'), may hold values from 0.25 to 1.75
- gate_values: bfloat16 [32768, 8192], P('seq', 'tp'), may hold values from -0.5 to 2
- se_filter: float32 [7, 8192], P(None, 'tp'), may hold values from -0.2 to 1
- mr_filter: bfloat16 [128, 8192], P(None, 'tp'), may hold values from -0.4 to 0.4
- band_offsets: int32 [64], P('tp'), may hold values from 0 to 1, as said below
- cotangent: bfloat16 [32768, 8192], P('seq', 'tp'), may hold values from -5 to 5
Outputs:
- output: bfloat16 [32768, 8192], P('seq', 'tp')
- input_grad: bfloat16 [32768, 8192], P('seq', 'tp')
- gain_grad: float32 [8192], P('tp')
- se_grad: float32 [7, 8192], P(None, 'tp')
- mr_grad: bfloat16 [128, 8192], P(None, 'tp')
Inputs may be any that keep to these rules, and one draw needn't show every extreme that they name: `band_offsets`: exactly half of the 64 groups have offset 1.
All inputs are finite; a program needn't handle non-finite values.
Results may differ from a plain program's by a relative error of at most 0.0054.
Values may be sent and summed in bfloat16 or wider, within the bound.
A program may use at most 128 MiB of HBM per device.

v0:
```python
import math

import jax
import jax.numpy as jnp
from jax import lax
from jax.sharding import PartitionSpec as P

D = 8192


def from_behind(value, axis, by):
    length = lax.axis_size(axis)
    pairs = [(i, i + by) for i in range(length) if 0 <= i + by < length]
    return lax.ppermute(value, axis, pairs)


def depthwise(lhs_rows, kernel_rows):
    result = lax.conv_general_dilated(
        lhs_rows[None],
        kernel_rows[:, None, :],
        window_strides=(1,),
        padding="VALID",
        dimension_numbers=("NWC", "WIO", "NWC"),
        feature_group_count=lhs_rows.shape[1],
        preferred_element_type=jnp.float32,
    )
    return result[0]


def short_filter(extended, se_filter):
    se_count = se_filter.shape[0]
    edge_count = se_count - 1
    out_rows = extended.shape[0] - edge_count
    running = jnp.zeros((out_rows, extended.shape[1]), jnp.float32)
    for tap_index in range(se_count):
        running = running + se_filter[tap_index][None, :] * extended[
            edge_count - tap_index : edge_count - tap_index + out_rows
        ].astype(jnp.float32)
    return running


def per_device(activations, norm_gain, gate_values, se_filter, mr_filter, band_offsets, cotangent):
    tok_rows, chan_count = activations.shape
    tap_count = mr_filter.shape[0]
    se_count = se_filter.shape[0]
    edge_count = se_count - 1
    kernel_span = 2 * tap_count
    act_float = activations.astype(jnp.float32)
    row_sq = lax.psum(jnp.sum(act_float * act_float, axis=1), "tp")
    inv_rms = lax.rsqrt(row_sq / D + 1e-06)[:, None]
    normed = act_float * inv_rms
    features = (normed * norm_gain[None, :]).astype(jnp.bfloat16)
    tail_rows = from_behind(features[tok_rows - edge_count :], "seq", 1)
    feat_ext = jnp.concatenate([tail_rows, features], axis=0)
    short_out = short_filter(feat_ext, se_filter).astype(jnp.bfloat16)
    prior_tail = from_behind(short_out[tok_rows - kernel_span + 1 :], "seq", 1)
    group_width = chan_count // band_offsets.shape[0]
    offsets = (band_offsets[:, None] + jnp.zeros((1, group_width), jnp.int32)).reshape(chan_count)
    upper_flag = offsets[None, :] == 1
    blank_rows = jnp.zeros((tap_count, chan_count), jnp.bfloat16)
    kernel = jnp.where(
        upper_flag,
        jnp.concatenate([blank_rows, mr_filter], axis=0),
        jnp.concatenate([mr_filter, blank_rows], axis=0),
    )
    short_ext = jnp.concatenate([prior_tail, short_out], axis=0)
    mixed_out = depthwise(short_ext, kernel[::-1])
    gate_float = gate_values.astype(jnp.float32)
    grad_out = cotangent.astype(jnp.float32)
    output = (gate_float * mixed_out).astype(jnp.bfloat16)
    grad_mix = (grad_out * gate_float).astype(jnp.bfloat16)
    later_mix = from_behind(grad_mix[: kernel_span - 1], "seq", -1)
    mix_ext = jnp.concatenate([grad_mix, later_mix], axis=0)
    back_grad = depthwise(mix_ext, kernel)
    kern_grad = depthwise(short_ext, grad_mix)[::-1]
    filter_grad = jnp.where(upper_flag, kern_grad[tap_count:], kern_grad[:tap_count])
    later_back = from_behind(back_grad[:edge_count].astype(jnp.bfloat16), "seq", -1).astype(
        jnp.float32
    )
    back_ext = jnp.concatenate([back_grad, later_back], axis=0)
    feat_grad = jnp.zeros((tok_rows, chan_count), jnp.float32)
    se_rows = []
    for tap_index in range(se_count):
        feat_grad = (
            feat_grad + se_filter[tap_index][None, :] * back_ext[tap_index : tap_index + tok_rows]
        )
        se_rows.append(
            jnp.sum(
                back_grad
                * feat_ext[edge_count - tap_index : edge_count - tap_index + tok_rows].astype(
                    jnp.float32
                ),
                axis=0,
            )
        )
    se_local = jnp.stack(se_rows, axis=0)
    gain_local = jnp.sum(feat_grad * normed, axis=0)
    scaled = feat_grad * norm_gain[None, :]
    inner_sum = lax.psum(jnp.sum(scaled * normed, axis=1), "tp")
    input_grad = (inv_rms * (scaled - normed * (inner_sum / D)[:, None])).astype(jnp.bfloat16)
    norm_scale = 1.0 / math.sqrt(tok_rows * lax.axis_size("seq"))
    filter_total, se_total, gain_total = lax.psum((filter_grad, se_local, gain_local), "seq")
    mr_grad = (filter_total * norm_scale).astype(jnp.bfloat16)
    return (output, input_grad, gain_total * norm_scale, se_total * norm_scale, mr_grad)


def solution(mesh):
    in_specs = (
        P("seq", "tp"),
        P("tp"),
        P("seq", "tp"),
        P(None, "tp"),
        P(None, "tp"),
        P("tp"),
        P("seq", "tp"),
    )
    out_specs = (P("seq", "tp"), P("seq", "tp"), P("tp"), P(None, "tp"), P(None, "tp"))
    return jax.shard_map(
        per_device, mesh=mesh, in_specs=in_specs, out_specs=out_specs, check_vma=False
    )
```

profile of v0, /device:TPU:1, one launch (start us, length us, event | category | flops | bytes accessed | tf_op | source)
XLA Modules:
  0.0 1987.2 jit_solution(9507306186312038888)
XLA Ops:
  7.3 4.5 fusion.11
  11.7 5.1 collective-permute-start.2
  17.4 6.0 psum.35
  26.1 14.5 collective-permute-done.2
  43.4 109.5 %fusion = f32[1,256,4096]{2,0,1:T(1,128)S(1)} fusion(bf16[1,511,4096]{2,1,0:T(8,128)(2,1)S(1)} %maximum_bitcast_fusion.1, bf16[256,1,4096]{2,0,1:T(8,128)(2,1)S(1)} %get-tuple-element.21), kind=kOutput, calls=%fused_computation.5 | convolution fusion | flops 536870912 | bytes 10477568 | tf_op jit(solution)/shard_map/conv_general_dilated | solution.py:18
  155.2 3.8 copy.68
  159.1 9.4 fusion.17
  168.6 5.5 psum.36
  174.0 5.7 fusion.16
  179.7 4.8 collective-permute-start
  185.8 3.9 fusion.25
  192.9 4.3 collective-permute-start.1
  197.2 30.5 %rev.4 = bf16[256,4096]{1,0:T(8,128)(2,1)} reverse(bf16[256,4096]{1,0:T(8,128)(2,1)} %get-tuple-element.22), dimensions={0} | reverse | bytes 4194304 | tf_op jit(solution)/shard_map/rev | solution.py:67
  227.7 546.5 %psum.37 = f32[4096]{0:T(1024)S(1)} all-reduce(f32[4096]{0:T(1024)S(1)} %get-tuple-element.11), channel_id=1, replica_groups=mesh['seq'=128,'tp'=2] {'seq'}, use_global_device_ids=true, to_apply=%region_5.6 | all-reduce | flops 4096 | bytes 32768 | tf_op jit(solution)/shard_map/psum | solution.py:102
  774.8 5.7 fusion.32
  786.3 110.0 %fusion.2 = f32[1,256,4096]{2,0,1:T(1,128)S(1)} fusion(bf16[1,511,4096]{2,1,0:T(8,128)(2,1)S(1)} %maximum_bitcast_fusion, bf16[256,1,4096]{2,0,1:T(8,128)(2,1)} %bitcast.19), kind=kOutput, calls=%fused_computation.7 | convolution fusion | flops 536870912 | bytes 10477568 | tf_op jit(solution)/shard_map/conv_general_dilated | solution.py:18
  896.3 3.8 fusion.60
  900.1 5.1 copy_bitcast_fusion.1
  905.3 16.7 slice.127
  921.9 10.3 slice.130
  932.2 4.0 broadcast_select_fusion
  936.3 111.3 %fusion.4 = f32[1,256,4096]{2,0,1:T(1,128)S(1)} fusion(bf16[1,511,4096]{2,1,0:T(8,128)(2,1)} %copy-done.5, bf16[256,1,4096]{2,0,1:T(8,128)(2,1)S(1)} %bitcast.52), kind=kOutput, calls=%fused_computation.9 | convolution fusion | flops 536870912 | bytes 10477568 | tf_op jit(solution)/shard_map/conv_general_dilated | solution.py:18
  1047.6 3.9 fusion.10
  1051.5 924.5 %all-reduce.5.cloned.1.call-done = (f32[7,4096]{1,0:T(8,128)}, f32[128,4096]{1,0:T(8,128)}) async-done(((f32[7,4096]{1,0:T(8,128)}, f32[128,4096]{1,0:T(8,128)}), (f32[7,4096]{1,0:T(8,128)}, f32[128,4096]{1,0:T(8,128)})) %all-reduce.5.cloned.1.call-update) | async-done | bytes 2211856 | tf_op jit(solution)/shard_map/psum | solution.py:102
  (66 shorter events, 23.4 us)
Async XLA Ops:
  7.2 9.7 copy-start.1
  7.2 10.2 copy-start.20
  7.2 16.3 copy-start.15
  7.2 17.0 copy-start.7
  7.2 1968.8 %all-reduce.5.cloned.1.call-start = ((), (), s32[]{:S(2)}) async-start(), calls=%async_computation | async-start | bytes 4456448 | tf_op jit(solution)/shard_map/psum | solution.py:102
  11.7 29.0 %collective-permute-start.2 = (bf16[255,4096]{1,0:T(8,128)(2,1)}, bf16[255,4096]{1,0:T(8,128)(2,1)}, u32[]{:S(2)}, u32[]{:S(2)}) collective-permute-start(bf16[255,4096]{1,0:T(8,128)(2,1)} %bitcast.50), channel_id=1, source_target_pairs={{2,0},{4,2},{6,4},{8,6},{10,8},{12,10},{14,12},{16,14},{18,16},{20... | collective-permute-start | bytes 6266888 | tf_op jit(solution)/shard_map/ppermute | solution.py:14
  23.5 2.7 copy-start.17
  43.4 111.6 %copy-start.19 = (f32[256]{0:T(256)S(1)}, f32[256]{0:T(256)}, u32[]{:S(2)}) copy-start(f32[256]{0:T(256)} %psum.35) | copy-start | bytes 3076
  153.0 6.0 copy-start.3
  153.1 5.9 collective-permute-start.3
  155.1 4.0 copy-start.2
  155.1 4.0 copy-start.8
  155.1 4.0 copy-start.9
  155.1 4.0 copy-start.10
  155.1 4.0 copy-start.11
  155.1 4.0 copy-start.12
  155.1 4.0 copy-start.13
  155.1 4.0 copy-start.14
  155.2 4.0 copy-start.16
  179.7 6.1 collective-permute-start
  192.9 588.5 %collective-permute-start.1 = (bf16[255,4096]{1,0:T(8,128)(2,1)}, bf16[255,4096]{1,0:T(8,128)(2,1)}, u32[]{:S(2)}, u32[]{:S(2)}) collective-permute-start(bf16[255,4096]{1,0:T(8,128)(2,1)} %slice.142), channel_id=1, source_target_pairs={{0,2},{2,4},{4,6},{6,8},{8,10},{10,12},{12,14},{14,16},{16,18},{18... | collective-permute-start | bytes 6266888 | tf_op jit(solution)/shard_map/ppermute | solution.py:14
  905.3 27.0 %copy-start.18 = (pred[4096]{0:T(1024)(128)(4,1)S(1)}, pred[4096]{0:T(1024)(128)(4,1)}, u32[]{:S(2)}) copy-start(pred[4096]{0:T(1024)(128)(4,1)} %copy-done.17) | copy-start | bytes 12292
  932.2 4.1 copy-start.6
  936.3 111.3 %copy-start.4 = (bf16[256,4096]{1,0:T(8,128)(2,1)S(1)}, bf16[256,4096]{1,0:T(8,128)(2,1)}, u32[]{:S(2)}) copy-start(bf16[256,4096]{1,0:T(8,128)(2,1)} %param.9) | copy-start | bytes 6291460
  (2 other events, 3.3 us)
Sparse Core Ops, SparseCore 0:
  936.4 1039.5 all-reduce.4
where the time goes:
time: 1990 us
  waiting for transfers between devices  940 us (47%)
  blocking collectives  558 us (28%)
  matrix products  331 us (17%)
  local copies, waits for them, and re-layouts  77.2 us (4%)
  other arithmetic  50.2 us (3%)
    psum x1, waiting for transfers between devices, per_device(): lax.psum((filter_grad, se_local, gain_local), 'seq')  924 us
    psum x1, blocking collectives, per_device(): lax.psum((filter_grad, se_local, gain_local), 'seq')  547 us
    conv_general_dilated x3, matrix products, depthwise(): lax.conv_general_dilated(lhs_rows[None], kernel_rows[:, None, :], window_...  331 us
  transfers between devices with their start and end apart: 5, of which 3 were waited for; matrix products, arithmetic and copies ran while one was open for 8% of the time, Pallas kernels for 0%

commit v1 on v0

v1 whole, which is shorter than its diff:
```python
import functools
import math

import jax
import jax.numpy as jnp
import numpy as np
from jax import lax
from jax.experimental import pallas as pl
from jax.experimental.pallas import tpu as pltpu
from jax.sharding import PartitionSpec as P

MESH = pl.DeviceIdType.MESH
CH = 256
BLK = 128
F32 = jnp.float32
BF16 = jnp.bfloat16


def transforms():
    angle = np.pi * (2 * np.arange(BLK)[:, None] + 1) * np.arange(2 * BLK)[None, :] / (2 * BLK)
    forward = np.concatenate([np.cos(angle), -np.sin(angle)], axis=0)
    inverse = forward.T / BLK
    return (
        jnp.asarray(forward, BF16),
        jnp.asarray(inverse[BLK:], BF16),
        jnp.asarray(inverse[:BLK], BF16),
    )


def dot(a, b):
    return jnp.dot(a, b, preferred_element_type=F32)


def remote(src, dst, send_sem, recv_sem, device):
    return pltpu.make_async_remote_copy(
        src_ref=src, dst_ref=dst, send_sem=send_sem, recv_sem=recv_sem,
        device_id=device, device_id_type=MESH,
    )


def both(x):
    return jnp.concatenate([x, x], axis=1)


def fold(x):
    return jnp.sum(x.reshape(x.shape[0] // 8, 8, x.shape[1]), axis=0)


def kernel(
    pn, zn, seq_size, dim, scale,
    act_h, gain_ref, gate_h, se_ref, mrf_h, off_ref, cot_h, fwd_ref, inv_hi_ref, inv_lo_ref,
    out_h, ig_h, gg_ref, seg_ref, mr_h,
    act, gate, cot, mrf, g_own, g_halo, s_own, s_halo, f_ext, tail_in, b_ext, head_in, spec,
    out_v, ig_v, row_acc, row_out, row_in, inv_rms, row2_out, row2_in,
    red, core_in, xy_out, xys_out, xy_in, xys_in, own_sum, z_out, z_in, mr_all, sg_all,
    in_sem, out_sem, g_send, g_recv, s_send, s_recv, edge_send, edge_recv, row_send, row_recv,
    core_send, core_recv, xy_send, xy_recv, xys_send, xys_recv, z_send, z_recv,
    zg_send, zg_recv, xg_send, xg_recv, xgs_send, xgs_recv, cg_send, cg_recv,
):
    nc = act.shape[0]
    rows = act.shape[1]
    seq = lax.axis_index("seq")
    tp = lax.axis_index("tp")
    core = lax.rem(seq, 2)
    z = lax.rem(seq // 2, zn)
    xy = seq // (2 * zn)
    after = (lax.rem(seq + 1, seq_size), tp)
    before = (lax.rem(seq + seq_size - 1, seq_size), tp)
    pair = (seq, 1 - tp)
    other_core = (seq + 1 - 2 * core, tp)

    def xy_peer(p):
        return (p * (2 * zn) + z * 2 + core, tp)

    def z_peer(j):
        return (xy * (2 * zn) + j * 2 + core, tp)

    def lanes(c):
        return pl.ds(pl.multiple_of(c * CH, CH), CH)

    def in_copy(n, c):
        src, dst = ((act_h, act), (gate_h, gate), (cot_h, cot), (mrf_h, mrf))[n]
        return pltpu.make_async_copy(src.at[:, lanes(c)], dst.at[c], in_sem.at[n, c])

    def loop(body, count=nc):
        def step(c, carry):
            body(c)
            return carry

        lax.fori_loop(0, count, step, 0)

    for n in range(4):
        loop(lambda c, n=n: in_copy(n, c).start())

    barrier = pltpu.get_barrier_semaphore()
    partners = [after, before, pair, other_core]
    partners += [xy_peer(lax.rem(xy + d, pn)) for d in range(1, pn)]
    partners += [z_peer(lax.rem(z + d, zn)) for d in range(1, zn)]
    for partner in partners:
        pl.semaphore_signal(barrier, inc=1, device_id=partner, device_id_type=MESH)
    pl.semaphore_wait(barrier, len(partners))

    row_acc[...] = jnp.zeros_like(row_acc)

    def squares(c):
        in_copy(0, c).wait()
        a = act[c].astype(F32)
        a = a * a
        row_acc[...] += a[:, :BLK] + a[:, BLK:]

    loop(squares)
    row_out[...] = jnp.broadcast_to(jnp.sum(row_acc[...], axis=1, keepdims=True), row_out.shape)
    row_copy = remote(row_out, row_in, row_send.at[0], row_recv.at[0], pair)
    row_copy.start()

    def g_copy(c):
        return remote(g_own.at[c], g_halo.at[c], g_send.at[c], g_recv.at[c], before)

    def gated(c):
        in_copy(1, c).wait()
        in_copy(2, c).wait()
        g_own[c] = (cot[c].astype(F32) * gate[c].astype(F32)).astype(BF16)
        g_copy(c).start()

    loop(gated)

    row_copy.wait()
    inv_rms[...] = lax.rsqrt((row_out[...] + row_in[...]) / dim + 1e-06)

    def featured(c):
        inv = both(inv_rms[...])
        f = (act[c].astype(F32) * inv * gain_ref[:, lanes(c)]).astype(BF16)
        f_ext[c, 8:, :] = f.astype(F32)

    loop(featured)
    tail_copy = remote(
        f_ext.at[:, pl.ds(rows, 8), :], tail_in, edge_send.at[0], edge_recv.at[0], after
    )
    tail_copy.start()

    def filtered(c):
        in_copy(3, c).wait()
        spec[c] = dot(fwd_ref[:, :BLK], mrf[c])

    loop(filtered)

    tail_copy.wait()

    @pl.when(seq == 0)
    def _():
        tail_in[...] = jnp.zeros_like(tail_in)

    def s_copy(c):
        return remote(s_own.at[c], s_halo.at[c], s_send.at[c], s_recv.at[c], after)

    def short(c):
        f_ext[c, :8, :] = tail_in[c]
        taps = se_ref[:, lanes(c)]
        for r in range(0, rows, 64):
            total = taps[0:1] * f_ext[c, 8 + r : 72 + r, :]
            for k in range(1, 7):
                total = total + taps[k : k + 1] * f_ext[c, 8 + r - k : 72 + r - k, :]
            s_own[c, r : r + 64, :] = total.astype(BF16)
        s_copy(c).start()

    loop(short)

    def upper(c):
        left = jnp.full((BLK, BLK), off_ref[2 * c], jnp.int32)
        right = jnp.full((BLK, BLK), off_ref[2 * c + 1], jnp.int32)
        return jnp.concatenate([left, right], axis=1).astype(F32).astype(BF16) > 0.5

    def backward(c):
        g_copy(c).wait()

        @pl.when(seq == seq_size - 1)
        def _():
            g_halo[c] = jnp.zeros_like(g_halo[c])

        up = upper(c)
        g0, g1 = g_own[c, :BLK], g_own[c, BLK:]
        g2, g3 = g_halo[c, :BLK], g_halo[c, BLK:]
        v0, v1, v2 = jnp.where(up, g1, g0), jnp.where(up, g2, g1), jnp.where(up, g3, g2)
        hr, hi = spec[c, :BLK], spec[c, BLK:]
        for n, window in enumerate(((v0, v1), (v1, v2))):
            v = dot(fwd_ref[...], jnp.concatenate(window, axis=0))
            vr, vi = v[:BLK], v[BLK:]
            prod = jnp.concatenate([hr * vr + hi * vi, hr * vi - hi * vr], axis=0).astype(BF16)
            b_ext[c, n * BLK : (n + 1) * BLK, :] = dot(inv_lo_ref[...], prod)

    loop(backward)
    head_copy = remote(
        b_ext.at[:, pl.ds(0, 8), :], head_in, edge_send.at[1], edge_recv.at[1], before
    )
    head_copy.start()

    def out_copy(c):
        return pltpu.make_async_copy(out_v.at[c], out_h.at[:, lanes(c)], out_sem.at[0, c])

    def forward(c):
        s_copy(c).wait()

        @pl.when(seq == 0)
        def _():
            s_halo[c] = jnp.zeros_like(s_halo[c])

        up = upper(c)
        s0, s1 = s_halo[c, :BLK], s_halo[c, BLK:]
        s2, s3 = s_own[c, :BLK], s_own[c, BLK:]
        w0, w1, w2 = jnp.where(up, s0, s1), jnp.where(up, s1, s2), jnp.where(up, s2, s3)
        hr, hi = spec[c, :BLK], spec[c, BLK:]
        kr, ki = 0.0, 0.0
        for n, window in enumerate(((w0, w1), (w1, w2))):
            at = slice(n * BLK, (n + 1) * BLK)
            w = dot(fwd_ref[...], jnp.concatenate(window, axis=0))
            wr, wi = w[:BLK], w[BLK:]
            q = dot(fwd_ref[:, BLK:], g_own[c, at])
            qr, qi = q[:BLK], q[BLK:]
            kr = kr + (wr * qr + wi * qi)
            ki = ki + (wr * qi - wi * qr)
            prod = jnp.concatenate([hr * wr - hi * wi, hr * wi + hi * wr], axis=0).astype(BF16)
            y = dot(inv_hi_ref[...], prod)
            out_v[c, at] = (gate[c, at].astype(F32) * y).astype(BF16)
        kk = jnp.concatenate([kr, ki], axis=0)
        top = kk.astype(BF16)
        low = (kk - top.astype(F32)).astype(BF16)
        red[c, :BLK, :] = dot(inv_lo_ref[...], top) + dot(inv_lo_ref[...], low)
        out_copy(c).start()

    loop(forward)

    head_copy.wait()

    @pl.when(seq == seq_size - 1)
    def _():
        head_in[...] = jnp.zeros_like(head_in)

    row_acc[...] = jnp.zeros_like(row_acc)

    def back_short(c):
        b_ext[c, rows:, :] = head_in[c]
        taps = se_ref[:, lanes(c)]
        gain = gain_ref[:, lanes(c)]
        sums = [jnp.zeros((8, CH), F32)] * 8
        for r in range(0, rows, 64):
            at = slice(r, r + 64)
            b = b_ext[c, at, :]
            grad = taps[0:1] * b
            for k in range(1, 7):
                grad = grad + taps[k : k + 1] * b_ext[c, r + k : r + k + 64, :]
            for k in range(7):
                sums[k] = sums[k] + fold(b * f_ext[c, 8 + r - k : 72 + r - k, :])
            normed = act[c, at].astype(F32) * both(inv_rms[at])
            sums[7] = sums[7] + fold(grad * normed)
            scaled = grad * gain
            inner = scaled * normed
            row_acc[at] += inner[:, :BLK] + inner[:, BLK:]
            spec[c, at, :] = scaled
        for k in range(8):
            red[c, BLK + k : BLK + k + 1, :] = jnp.sum(sums[k], axis=0, keepdims=True)

    loop(back_short)
    row2_out[...] = jnp.broadcast_to(jnp.sum(row_acc[...], axis=1, keepdims=True), row2_out.shape)
    row2_copy = remote(row2_out, row2_in, row_send.at[1], row_recv.at[1], pair)
    row2_copy.start()

    core_copy = remote(
        red.at[pl.ds((1 - core) * pn, pn)], core_in, core_send.at[0], core_recv.at[0], other_core
    )
    core_copy.start()

    row2_copy.wait()
    row2_in[...] = (row2_out[...] + row2_in[...]) / dim

    def ig_copy(c):
        return pltpu.make_async_copy(ig_v.at[c], ig_h.at[:, lanes(c)], out_sem.at[1, c])

    def finish(c):
        inv = both(inv_rms[...])
        normed = act[c].astype(F32) * inv
        ig_v[c] = (inv * (spec[c] - normed * both(row2_in[...]))).astype(BF16)
        ig_copy(c).start()

    loop(finish)

    core_copy.wait()

    def xy_copy(p):
        return remote(xy_out.at[p], xy_in.at[xy], xy_send.at[p], xy_recv.at[xy], xy_peer(p))

    def xys_copy(p):
        return remote(xys_out.at[p], xys_in.at[xy], xys_send.at[p], xys_recv.at[xy], xy_peer(p))

    for d in range(1, pn):
        p = lax.rem(xy + d, pn)
        q = red[core * pn + p] + core_in[p]
        xy_out[p] = q[:BLK].astype(BF16)
        xys_out[p] = q[BLK:]
        xy_copy(p).start()
        xys_copy(p).start()
    own_sum[...] = red[core * pn + xy] + core_in[xy]
    for d in range(1, pn):
        p = lax.rem(xy + d, pn)
        xy_copy(p).wait_send()
        xys_copy(p).wait_send()
        remote(xy_out.at[p], xy_in.at[p], xy_send.at[p], xy_recv.at[p], xy_peer(p)).wait_recv()
        remote(xys_out.at[p], xys_in.at[p], xys_send.at[p], xys_recv.at[p], xy_peer(p)).wait_recv()
        own_sum[:BLK, :] += xy_in[p].astype(F32)
        own_sum[BLK:, :] += xys_in[p]

    part = BLK // zn
    for j in range(zn):
        z_out[j, :part, :] = own_sum[j * part : (j + 1) * part, :]
        z_out[j, part:, :] = own_sum[BLK:, :]

    def z_copy(j):
        return remote(z_out.at[j], z_in.at[z], z_send.at[j], z_recv.at[z], z_peer(j))

    for d in range(1, zn):
        z_copy(lax.rem(z + d, zn)).start()
    z_in[z] = z_out[z]
    for d in range(1, zn):
        j = lax.rem(z + d, zn)
        z_copy(j).wait_send()
        remote(z_out.at[j], z_in.at[j], z_send.at[j], z_recv.at[j], z_peer(j)).wait_recv()
    total = z_in[0]
    for j in range(1, zn):
        total = total + z_in[j]
    total = total * scale

    mine = core * pn + xy
    mr_all[mine, pl.ds(pl.multiple_of(z * part, part), part), :] = total[:part].astype(BF16)
    sg_all[mine] = total[part:]

    def piece(j):
        return mr_all.at[mine, pl.ds(pl.multiple_of(j * part, part), part), :]

    for d in range(1, zn):
        j = lax.rem(z + d, zn)
        remote(piece(z), piece(z), zg_send.at[j], zg_recv.at[z], z_peer(j)).start()
    for d in range(1, zn):
        j = lax.rem(z + d, zn)
        remote(piece(z), piece(z), zg_send.at[j], zg_recv.at[z], z_peer(j)).wait_send()
        remote(piece(j), piece(j), zg_send.at[j], zg_recv.at[j], z_peer(j)).wait_recv()

    for d in range(1, pn):
        p = lax.rem(xy + d, pn)
        remote(mr_all.at[mine], mr_all.at[mine], xg_send.at[p], xg_recv.at[xy], xy_peer(p)).start()
        remote(sg_all.at[mine], sg_all.at[mine], xgs_send.at[p], xgs_recv.at[xy], xy_peer(p)).start()
    for d in range(1, pn):
        p = lax.rem(xy + d, pn)
        theirs = core * pn + p
        remote(mr_all.at[mine], mr_all.at[mine], xg_send.at[p], xg_recv.at[xy], xy_peer(p)).wait_send()
        remote(sg_all.at[mine], sg_all.at[mine], xgs_send.at[p], xgs_recv.at[xy], xy_peer(p)).wait_send()
        remote(mr_all.at[theirs], mr_all.at[theirs], xg_send.at[p], xg_recv.at[p], xy_peer(p)).wait_recv()
        remote(sg_all.at[theirs], sg_all.at[theirs], xgs_send.at[p], xgs_recv.at[p], xy_peer(p)).wait_recv()

    def halves(n, ref, k):
        half = ref.at[pl.ds(k * pn, pn)]
        return remote(half, half, cg_send.at[n], cg_recv.at[n], other_core)

    for n, ref in enumerate((mr_all, sg_all)):
        halves(n, ref, core).start()
    for n, ref in enumerate((mr_all, sg_all)):
        halves(n, ref, core).wait_send()
        halves(n, ref, 1 - core).wait_recv()

    def mr_copy(c):
        return pltpu.make_async_copy(mr_all.at[c], mr_h.at[:, lanes(c)], out_sem.at[2, c])

    def spread(c):
        mr_copy(c).start()
        seg_ref[:, lanes(c)] = sg_all[c, :7, :]
        gg_ref[:, lanes(c)] = sg_all[c, 7:8, :]

    loop(spread)

    def drain(c):
        out_copy(c).wait()
        ig_copy(c).wait()
        mr_copy(c).wait()

    loop(drain)


def per_device(seq_size, dim, tokens, act, gain, gate, se, mrf, off, cot):
    rows, chans = act.shape
    nc = chans // CH
    zn = 8 if seq_size == 128 else 2
    pn = seq_size // (2 * zn)
    assert nc == 2 * pn and rows == 2 * BLK and mrf.shape[0] == BLK and se.shape[0] == 7
    fwd, inv_hi, inv_lo = transforms()
    any_spec = pl.BlockSpec(memory_space=pl.ANY)
    vmem = pl.BlockSpec(memory_space=pltpu.VMEM)
    smem = pl.BlockSpec(memory_space=pltpu.SMEM)
    dma = pltpu.SemaphoreType.DMA
    part = BLK // zn
    V = pltpu.VMEM
    scratch = [
        V((nc, rows, CH), BF16), V((nc, rows, CH), BF16), V((nc, rows, CH), BF16), V((nc, BLK, CH), BF16),
        V((nc, rows, CH), BF16), V((nc, rows, CH), BF16), V((nc, rows, CH), BF16), V((nc, rows, CH), BF16),
        V((nc, rows + 8, CH), F32), V((nc, 8, CH), F32), V((nc, rows + 8, CH), F32), V((nc, 8, CH), F32),
        V((nc, rows, CH), F32),
        V((nc, rows, CH), BF16), V((nc, rows, CH), BF16),
        V((rows, BLK), F32), V((rows, BLK), F32), V((rows, BLK), F32), V((rows, BLK), F32),
        V((rows, BLK), F32), V((rows, BLK), F32),
        V((nc, BLK + 8, CH), F32), V((pn, BLK + 8, CH), F32),
        V((pn, BLK, CH), BF16), V((pn, 8, CH), F32), V((pn, BLK, CH), BF16), V((pn, 8, CH), F32),
        V((BLK + 8, CH), F32), V((zn, part + 8, CH), F32), V((zn, part + 8, CH), F32),
        V((nc, BLK, CH), BF16), V((nc, 8, CH), F32),
        dma((4, nc)), dma((3, nc)), dma((nc,)), dma((nc,)), dma((nc,)), dma((nc,)),
        dma((2,)), dma((2,)), dma((2,)), dma((2,)),
        dma((1,)), dma((1,)), dma((pn,)), dma((pn,)), dma((pn,)), dma((pn,)),
        dma((zn,)), dma((zn,)), dma((zn,)), dma((zn,)),
        dma((pn,)), dma((pn,)), dma((pn,)), dma((pn,)), dma((2,)), dma((2,)),
    ]
    out, ig, gg, seg, mr = pl.pallas_call(
        functools.partial(kernel, pn, zn, seq_size, dim, 1.0 / math.sqrt(tokens)),
        out_shape=(
            jax.ShapeDtypeStruct((rows, chans), BF16),
            jax.ShapeDtypeStruct((rows, chans), BF16),
            jax.ShapeDtypeStruct((1, chans), F32),
            jax.ShapeDtypeStruct((7, chans), F32),
            jax.ShapeDtypeStruct((BLK, chans), BF16),
        ),
        in_specs=[any_spec, vmem, any_spec, vmem, any_spec, smem, any_spec, vmem, vmem, vmem],
        out_specs=(any_spec, any_spec, vmem, vmem, any_spec),
        scratch_shapes=scratch,
        compiler_params=pltpu.CompilerParams(
            collective_id=0, has_side_effects=True, vmem_limit_bytes=58 * 1024 * 1024
        ),
        name="hyena",
    )(act, gain.reshape(1, chans), gate, se, mrf, off, cot, fwd, inv_hi, inv_lo)
    return out, ig, gg.reshape(chans), seg, mr


def solution(mesh):
    in_specs = (
        P("seq", "tp"), P("tp"), P("seq", "tp"), P(None, "tp"), P(None, "tp"), P("tp"), P("seq", "tp"),
    )
    out_specs = (P("seq", "tp"), P("seq", "tp"), P("tp"), P(None, "tp"), P(None, "tp"))

    def whole(act, *rest):
        tokens, dim = act.shape
        body = functools.partial(per_device, mesh.shape["seq"], dim, tokens)
        return jax.shard_map(
            body, mesh=mesh, in_specs=in_specs, out_specs=out_specs, check_vma=False
        )(act, *rest)

    return whole
```

time: 1990 us -> 120 us (0.06)
  waiting for transfers between devices: 940 us -> 0 us
  blocking collectives: 558 us -> 0 us
  matrix products: 331 us -> 0 us
  Pallas kernels: 0 us -> 113 us
  local copies, waits for them, and re-layouts: 77.2 us -> 6.85 us
  other arithmetic: 50.2 us -> 0 us
    psum x1 -> x0, waiting for transfers between devices: 924 us -> none  [per_device(): lax.psum((filter_grad, se_local, gain_local), 'seq')]
    psum x3 -> x0, blocking collectives: 558 us -> none  [the longest x1 547 us: per_device(): lax.psum((filter_grad, se_local, gain_local), 'seq')]
    conv_general_dilated x3 -> x0, matrix products: 331 us -> none  [depthwise(): lax.conv_general_dilated(lhs_rows[None], kernel_rows[:, None, :], window_...]
    pallas_call x0 -> x1, Pallas kernels: none -> 113 us  [per_device(): pl.pallas_call(functools.partial(kernel, pn, zn, seq_size, dim, 1.0 / mat...]
    slice x8 -> x0, local copies, waits for them, and re-layouts: 38.5 us -> none  [the longest x2 21.8 us: per_device(): kern_grad[tap_count:]]
    rev x1 -> x0, local copies, waits for them, and re-layouts: 30.5 us -> none  [per_device(): mixed_out = depthwise(short_ext, kernel[::-1])]
    convert_element_type x6 -> x0, other arithmetic: 20.7 us -> none  [the longest x1 5.68 us: per_device(): (inv_rms * (scaled - normed * (inner_sum / D)[:, None])).astype(jnp.bfloa...]
  transfers between devices with their start and end apart: 5 -> 0, of which waited for: 3 -> 0; matrix products, arithmetic and copies ran while one was open for 8% -> 0% of each run, Pallas kernels for 0% -> 0%
where the time goes in v1:
time: 120 us
  Pallas kernels  113 us (94%)
  local copies, waits for them, and re-layouts  6.85 us (6%)
    pallas_call x1, Pallas kernels, per_device(): pl.pallas_call(functools.partial(kernel, pn, zn, seq_size, dim, 1.0 / mat...  113 us
    unnamed x13, local copies, waits for them, and re-layouts  6.85 us

profile of v1, /device:TPU:1, one launch (start us, length us, event | category | flops | bytes accessed | tf_op | source)
XLA Modules:
  0.0 120.1 jit_solution(11325729364920148521)
XLA Ops:
  0.6 112.6 %hyena.1 = (bf16[256,4096]{1,0:T(8,128)(2,1)}, bf16[256,4096]{1,0:T(8,128)(2,1)}, f32[1,4096]{1,0:T(1,128)}, f32[7,4096]{1,0:T(8,128)}, bf16[128,4096]{1,0:T(8,128)(2,1)}) custom-call(bf16[256,4096]{1,0:T(8,128)(2,1)} %act_h.1, f32[1,4096]{1,0:T(1,128)} %bitcast.2, bf16[256,4096]{1,0:T(8,128)(2,1)} %gate_h.1, f32[7,4096]{1,0:T(8,128)} %se_ref.1, ...), custom_call_target="tpu_custom_call" | custom-call | tf_op jit(solution)/shard_map/hyena/pallas_call | solution.py:417
  113.3 0.0 copy-start
  113.3 3.3 %copy.20 = bf16[256,4096]{1,0:T(8,128)(2,1)} copy(bf16[256,4096]{1,0:T(8,128)(2,1)} %get-tuple-element.20) | data formatting | bytes 4194304
  116.5 0.0 copy-done
  116.5 0.0 copy-start.3
  116.5 0.0 copy-start.2
  116.6 0.0 copy-start.1
  116.6 1.3 %copy.21 = bf16[256,4096]{1,0:T(8,128)(2,1)} copy(bf16[256,4096]{1,0:T(8,128)(2,1)S(1)} %copy-done) | data formatting | bytes 4194304
  117.9 0.0 copy-done.3
  117.9 0.6 copy.22
  118.5 0.0 copy-done.2
  118.5 0.7 copy.23
  119.1 0.0 copy-done.1
  119.2 1.0 copy.24
Async XLA Ops:
  113.3 3.3 %copy-start = (bf16[256,4096]{1,0:T(8,128)(2,1)S(1)}, bf16[256,4096]{1,0:T(8,128)(2,1)}, u32[]{:S(2)}) copy-start(bf16[256,4096]{1,0:T(8,128)(2,1)} %get-tuple-element.21) | copy-start | bytes 6291460
  116.5 1.3 %copy-start.3 = (f32[1,4096]{1,0:T(1,128)S(1)}, f32[1,4096]{1,0:T(1,128)}, u32[]{:S(2)}) copy-start(f32[1,4096]{1,0:T(1,128)} %get-tuple-element.12) | copy-start | bytes 49156
  116.5 1.9 %copy-start.2 = (f32[7,4096]{1,0:T(8,128)S(1)}, f32[7,4096]{1,0:T(8,128)}, u32[]{:S(2)}) copy-start(f32[7,4096]{1,0:T(8,128)} %get-tuple-element.23) | copy-start | bytes 344068
  116.6 2.6 %copy-start.1 = (bf16[128,4096]{1,0:T(8,128)(2,1)S(1)}, bf16[128,4096]{1,0:T(8,128)(2,1)}, u32[]{:S(2)}) copy-start(bf16[128,4096]{1,0:T(8,128)(2,1)} %get-tuple-element.24) | copy-start | bytes 3145732

commit v2 on v1

v2 whole, which is shorter than its diff:
```python
import functools
import math

import jax
import jax.numpy as jnp
import numpy as np
from jax import lax
from jax.experimental import pallas as pl
from jax.experimental.pallas import tpu as pltpu
from jax.sharding import PartitionSpec as P

MESH = pl.DeviceIdType.MESH
CH = 256
BLK = 128
SE = 7
LAGS = BLK + 8
LATE = 3
F32 = jnp.float32
BF16 = jnp.bfloat16


def transforms():
    angle = np.pi * (2 * np.arange(BLK)[:, None] + 1) * np.arange(2 * BLK)[None, :] / (2 * BLK)
    forward = np.concatenate([np.cos(angle), -np.sin(angle)], axis=0)
    inverse = forward.T / BLK
    return (
        jnp.asarray(forward, BF16),
        jnp.asarray(inverse[BLK:], BF16),
        jnp.asarray(np.concatenate([inverse[:LAGS], inverse[:LAGS]], axis=1), BF16),
    )


def dot(a, b):
    return jnp.dot(a, b, preferred_element_type=F32)


def remote(src, dst, send_sem, recv_sem, device):
    return pltpu.make_async_remote_copy(
        src_ref=src, dst_ref=dst, send_sem=send_sem, recv_sem=recv_sem,
        device_id=device, device_id_type=MESH,
    )


def both(x):
    return jnp.concatenate([x, x], axis=1)


def split(x):
    top = x.astype(BF16)
    return top, (x - top.astype(F32)).astype(BF16)


def kernel(
    pn, zn, seq_size, dim, scale,
    act_h, gain_ref, gate_h, se_ref, mrf_h, off_ref, cot_h, fwd_ref, inv_hi_ref, inv_lo_ref,
    out_h, ig_h, gg_ref, seg_ref, mr_h,
    act, gate, cot, mrf, g_own, g_halo, s_own, s_halo, zeros, f_own, f_ext, tail_out, tail_in, b_ext, head_in, spec,
    out_v, ig_v, row_acc, row_out, row_in, inv_rms, row2_out, row2_in, no_rows, mean2,
    red, core_in, xy_out, xy_in, own_sum, z_out, z_in, z_last_out, z_last_in, lags, mr_all,
    in_sem, out_sem, g_send, g_recv, s_send, s_recv, tail_send, tail_recv, head_send, head_recv, row_send, row_recv,
    core_send, core_recv, xy_send, xy_recv, z_send, z_recv, zl_send, zl_recv, zg_send, zg_recv, zgl_send, zgl_recv, xg_send, xg_recv, cg_send, cg_recv,
):
    nc = act.shape[0]
    rows = act.shape[1]
    seq = lax.axis_index("seq")
    tp = lax.axis_index("tp")
    core = lax.rem(seq, 2)
    z = lax.rem(seq // 2, zn)
    xy = seq // (2 * zn)
    first = seq == 0
    last = seq == seq_size - 1
    after = (lax.rem(seq + 1, seq_size), tp)
    before = (lax.rem(seq + seq_size - 1, seq_size), tp)
    pair = (seq, 1 - tp)
    other_core = (seq + 1 - 2 * core, tp)

    def xy_peer(p):
        return (p * (2 * zn) + z * 2 + core, tp)

    def z_peer(j):
        return (xy * (2 * zn) + j * 2 + core, tp)

    def turn(start, t):
        return lax.rem(start + pn - t, pn)

    before_xy = lax.rem(seq + seq_size - 1, seq_size) // (2 * zn)

    def lanes(c):
        return pl.ds(pl.multiple_of(c * CH, CH), CH)

    def in_copy(n, c):
        src, dst = ((act_h, act), (gate_h, gate), (cot_h, cot), (mrf_h, mrf))[n]
        return pltpu.make_async_copy(src.at[:, lanes(c)], dst.at[c], in_sem.at[n, c])

    def loop(body, start=0, stop=nc):
        def step(c, carry):
            body(c)
            return carry

        lax.fori_loop(start, stop, step, 0)

    barrier = pltpu.get_barrier_semaphore()
    partners = [after, before, pair, other_core]
    partners += [xy_peer(lax.rem(xy + d, pn)) for d in range(1, pn)]
    partners += [z_peer(lax.rem(z + d, zn)) for d in range(1, zn)]
    for partner in partners:
        pl.semaphore_signal(barrier, inc=1, device_id=partner, device_id_type=MESH)

    def fetch(t):
        i = turn(before_xy, t)
        for c in (2 * i, 2 * i + 1):
            in_copy(1, c).start()
            in_copy(2, c).start()

    pairs = nc // 2
    loop(lambda c: in_copy(0, c).start())
    loop(fetch, 0, pairs)
    loop(lambda c: in_copy(3, c).start())

    zeros[...] = jnp.zeros_like(zeros)
    no_rows[...] = jnp.zeros_like(no_rows)
    row_acc[...] = jnp.zeros_like(row_acc)

    def squares(c):
        in_copy(0, c).wait()
        a = act[c].astype(F32)
        a = a * a
        row_acc[...] += a[:, :BLK] + a[:, BLK:]

    def across(acc):
        return jnp.broadcast_to(jnp.sum(jnp.transpose(acc), axis=0, keepdims=True), (8, rows))

    def down(x):
        return jnp.broadcast_to(jnp.transpose(x)[:, :1], (rows, BLK))

    pl.semaphore_wait(barrier, len(partners))

    loop(squares)
    row_out[...] = across(row_acc[...])
    row_copy = remote(row_out, row_in, row_send.at[0], row_recv.at[0], pair)
    row_copy.start()

    def g_copy(c, src=None):
        return remote(g_own.at[c] if src is None else src, g_halo.at[c], g_send.at[c], g_recv.at[c], before)

    def gated(c):
        in_copy(1, c).wait()
        in_copy(2, c).wait()
        g_own[c] = (cot[c].astype(F32) * gate[c].astype(F32)).astype(BF16)

        @pl.when(first)
        def _():
            g_copy(c, zeros).start()

        @pl.when(jnp.logical_not(first))
        def _():
            g_copy(c).start()

    def gated_pair(t):
        i = turn(before_xy, t)
        for c in (2 * i, 2 * i + 1):
            gated(c)

    loop(gated_pair, 0, pairs)

    def filtered(i):
        for n in range(4):
            in_copy(3, 4 * i + n).wait()
        for n in range(4):
            spec[4 * i + n] = dot(fwd_ref[:, :BLK], mrf[4 * i + n])

    loop(filtered, 0, nc // 4)

    row_copy.wait()
    inv_rms[...] = down(lax.rsqrt((row_out[...] + row_in[...]) / dim + 1e-06))

    def feature(c, at):
        return (act[c, at].astype(F32) * both(inv_rms[at]) * gain_ref[:, lanes(c)]).astype(BF16)

    def tail(c):
        end = feature(c, slice(rows - 16, rows)).astype(F32)
        tail_out[c] = jnp.where(last, 0.0, end[8:])

    loop(tail)
    tail_copy = remote(tail_out, tail_in, tail_send.at[0], tail_recv.at[0], after)
    tail_copy.start()

    def short_rows(c, r, count):
        taps = se_ref[:, lanes(c)]
        total = taps[0:1] * f_ext[c, 8 + r : 8 + r + count, :]
        for k in range(1, SE):
            total = total + taps[k : k + 1] * f_ext[c, 8 + r - k : 8 + r + count - k, :]
        s_own[c, r : r + count, :] = total.astype(BF16)

    def featured(c):
        f = feature(c, slice(0, rows))
        f_own[c] = f
        f_ext[c, 8:, :] = f.astype(F32)
        short_rows(c, 16, 48)
        for r in range(64, rows, 64):
            short_rows(c, r, 64)

    loop(featured)
    tail_copy.wait()

    def s_copy(c, src=None):
        return remote(s_own.at[c] if src is None else src, s_halo.at[c], s_send.at[c], s_recv.at[c], after)

    def short(c):
        f_ext[c, :8, :] = tail_in[c]
        short_rows(c, 0, 16)

        @pl.when(last)
        def _():
            s_copy(c, zeros).start()

        @pl.when(jnp.logical_not(last))
        def _():
            s_copy(c).start()

    loop(short)

    def upper(c):
        left = jnp.full((BLK, BLK), off_ref[2 * c], jnp.int32)
        right = jnp.full((BLK, BLK), off_ref[2 * c + 1], jnp.int32)
        return jnp.concatenate([left, right], axis=1).astype(F32)

    def backward(c):
        flag = upper(c)
        up = flag.astype(BF16) > 0.5
        g0, g1 = g_own[c, :BLK], g_own[c, BLK:]
        g2, g3 = g_halo[c, :BLK], g_halo[c, BLK:]
        v0, v1, v2 = jnp.where(up, g1, g0), jnp.where(up, g2, g1), jnp.where(up, g3, g2)
        hr, hi = spec[c, :BLK], spec[c, BLK:]
        kr, ki = 0.0, 0.0
        for n, window in enumerate(((v0, v1), (v1, v2))):
            at = slice(n * BLK, (n + 1) * BLK)
            v = dot(fwd_ref[...], jnp.concatenate(window, axis=0))
            vr, vi = v[:BLK], v[BLK:]
            prod = jnp.concatenate([hr * vr + hi * vi, hr * vi - hi * vr], axis=0).astype(BF16)
            b_ext[c, at, :] = dot(inv_lo_ref[:BLK, : 2 * BLK], prod)
            s = dot(fwd_ref[:, :BLK], f_own[c, at])
            sr, si = s[:BLK], s[BLK:]
            kr = kr + (sr * vr + si * vi)
            ki = ki + (sr * vi - si * vr)
        top, low = split(jnp.concatenate([kr, ki], axis=0))
        x = dot(inv_lo_ref[...], jnp.concatenate([top, low], axis=0))
        red[c, :BLK, :] = x[:BLK]
        up8 = flag[:8] > 0.5
        f0 = f_own[c, BLK - 16 : BLK].astype(F32)[8:]
        f1 = f_own[c, rows - 16 : rows].astype(F32)[8:]
        fa, fb = jnp.where(up8, tail_in[c], f0), jnp.where(up8, f0, f1)
        ua = g0[:16].astype(F32)[:8] + g2[:16].astype(F32)[:8]
        ub = g1[:16].astype(F32)[:8] + g3[:16].astype(F32)[:8]
        row = lax.broadcasted_iota(jnp.int32, (8, CH), 0)
        fix = x[BLK:]
        for r in range(1, SE - 1):
            term = pltpu.roll(fa, r, 0) * ua + pltpu.roll(fb, r, 0) * ub
            term = jnp.sum(jnp.where(row < r, term, 0.0), axis=0, keepdims=True)
            fix = fix + jnp.where(row == r, term, 0.0)
        red[c, BLK:, :] = fix

    def head_copy(c, src=None):
        src = b_ext.at[c, pl.ds(0, 8), :] if src is None else src
        return remote(src, head_in.at[c], head_send.at[c], head_recv.at[c], before)

    def core_copy(i):
        return remote(red.at[2 * i + 1 - core], core_in.at[i], core_send.at[i], core_recv.at[i], other_core)

    def backward_pair(t):
        i = turn(xy, t)
        for c in (2 * i, 2 * i + 1):
            g_copy(c).wait_recv()
        for c in (2 * i, 2 * i + 1):
            backward(c)
        core_copy(i).start()
        for c in (2 * i, 2 * i + 1):

            @pl.when(first)
            def _(c=c):
                head_copy(c, no_rows).start()

            @pl.when(jnp.logical_not(first))
            def _(c=c):
                head_copy(c).start()

    def back_short(c):
        b_ext[c, rows:, :] = head_in[c]
        taps = se_ref[:, lanes(c)]
        gain = gain_ref[:, lanes(c)]
        for r in range(0, rows, 64):
            at = slice(r, r + 64)
            grad = taps[0:1] * b_ext[c, at, :]
            for k in range(1, SE):
                grad = grad + taps[k : k + 1] * b_ext[c, r + k : r + k + 64, :]
            scaled = grad * gain
            inner = scaled * (act[c, at].astype(F32) * both(inv_rms[at]))
            row_acc[at] += inner[:, :BLK] + inner[:, BLK:]
            f_ext[c, at, :] = scaled

    def back_short_pair(t):
        i = turn(xy, t)
        for c in (2 * i, 2 * i + 1):
            head_copy(c).wait_recv()
        for c in (2 * i, 2 * i + 1):
            back_short(c)

    def xy_copy(p):
        return remote(xy_out.at[p], xy_in.at[xy], xy_send.at[p], xy_recv.at[xy], xy_peer(p))

    def xy_start(t):
        i = turn(xy, t)
        core_copy(i).wait()
        q = red[2 * i + core] + core_in[i]

        @pl.when(i == xy)
        def _():
            own_sum[...] = q

        @pl.when(i != xy)
        def _():
            xy_out[i, :BLK, :] = q[:BLK].astype(BF16)
            top = q[BLK:].astype(BF16).astype(F32)
            xy_out[i, BLK:, :] = jnp.concatenate([top, q[BLK:] - top], axis=0).astype(BF16)
            xy_copy(i).start()

    def out_copy(c):
        return pltpu.make_async_copy(out_v.at[c], out_h.at[:, lanes(c)], out_sem.at[0, c])

    def forward(c):
        up = upper(c).astype(BF16) > 0.5
        s0, s1 = s_halo[c, :BLK], s_halo[c, BLK:]
        s2, s3 = s_own[c, :BLK], s_own[c, BLK:]
        w0, w1, w2 = jnp.where(up, s0, s1), jnp.where(up, s1, s2), jnp.where(up, s2, s3)
        hr, hi = spec[c, :BLK], spec[c, BLK:]
        for n, window in enumerate(((w0, w1), (w1, w2))):
            at = slice(n * BLK, (n + 1) * BLK)
            w = dot(fwd_ref[...], jnp.concatenate(window, axis=0))
            wr, wi = w[:BLK], w[BLK:]
            prod = jnp.concatenate([hr * wr - hi * wi, hr * wi + hi * wr], axis=0).astype(BF16)
            y = dot(inv_hi_ref[...], prod)
            out_v[c, at] = (gate[c, at].astype(F32) * y).astype(BF16)

    def forward_pair(i):
        for c in (2 * i, 2 * i + 1):
            s_copy(c).wait()
        for c in (2 * i, 2 * i + 1):
            forward(c)
        for c in (2 * i, 2 * i + 1):
            out_copy(c).start()

    part = BLK // zn
    end = zn - 1

    def z_copy(j):
        return remote(z_out.at[j], z_in.at[z], z_send.at[j], z_recv.at[z], z_peer(j))

    def z_last_copy():
        return remote(z_last_out, z_last_in.at[z], zl_send.at[0], zl_recv.at[z], z_peer(end))

    def z_start():
        for d in range(1, pn):
            p = lax.rem(xy + d, pn)
            remote(xy_out.at[p], xy_in.at[p], xy_send.at[p], xy_recv.at[p], xy_peer(p)).wait_recv()
        total = own_sum[...]
        for d in range(1, pn):
            x = xy_in[lax.rem(xy + d, pn)].astype(F32)
            total = total + jnp.concatenate([x[:BLK], x[BLK : BLK + 8] + x[BLK + 8 :]], axis=0)
        for j in range(zn):
            z_out[j] = total[j * part : (j + 1) * part]
        z_last_out[...] = total[BLK:]
        for d in range(1, zn):
            z_copy(lax.rem(z + d, zn)).start()

        @pl.when(z != end)
        def _():
            z_last_copy().start()

    def piece(j):
        return lags.at[pl.ds(pl.multiple_of(j * part, part), part), :]

    def zg_copy(i, j):
        return remote(piece(i), piece(i), zg_send.at[j], zg_recv.at[i], z_peer(j))

    def zg_last_copy(j):
        rest = lags.at[pl.ds(BLK, 8), :]
        return remote(rest, rest, zgl_send.at[j], zgl_recv.at[0], z_peer(j))

    def z_sum():
        total = z_out[z]
        for d in range(1, zn):
            j = lax.rem(z + d, zn)
            remote(z_out.at[j], z_in.at[j], z_send.at[j], z_recv.at[j], z_peer(j)).wait_recv()
            total = total + z_in[j]
        lags[pl.ds(pl.multiple_of(z * part, part), part), :] = total
        for d in range(1, zn):
            zg_copy(z, lax.rem(z + d, zn)).start()

        @pl.when(z == end)
        def _():
            rest = z_last_out[...]
            for j in range(zn - 1):
                remote(z_last_out, z_last_in.at[j], zl_send.at[0], zl_recv.at[j], z_peer(j)).wait_recv()
                rest = rest + z_last_in[j]
            lags[BLK:, :] = rest
            for j in range(zn - 1):
                zg_last_copy(j).start()

    def xg_copy(p, q):
        half = mr_all.at[p, core]
        return remote(half, half, xg_send.at[q], xg_recv.at[p], xy_peer(q))

    def grads_start():
        for d in range(1, zn):
            j = lax.rem(z + d, zn)
            zg_copy(z, j).wait_send()
            zg_copy(j, j).wait_recv()

        @pl.when(z != end)
        def _():
            z_last_copy().wait_send()
            zg_last_copy(end).wait_recv()

        @pl.when(z == end)
        def _():
            for j in range(zn - 1):
                zg_last_copy(j).wait_send()

        mine = 2 * xy + core
        taps = se_ref[:, lanes(mine)]
        filt = mrf[mine].astype(F32)
        grads = []
        kern = jnp.zeros((BLK, CH), F32)
        gain_sum = jnp.zeros((1, CH), F32)
        for k in range(SE):
            x = lags[k : k + BLK, :]
            kern = kern + taps[k : k + 1] * x
            grads.append(jnp.sum(filt * x, axis=0, keepdims=True) * scale)
            gain_sum = gain_sum + taps[k : k + 1] * grads[k]
        grads.append(gain_sum / gain_ref[:, lanes(mine)])
        grads = jnp.concatenate(grads, axis=0)
        top = grads.astype(BF16).astype(F32)
        mr_all[xy, core, :BLK, :] = (kern * scale).astype(BF16)
        mr_all[xy, core, BLK:, :] = jnp.concatenate([top, grads - top], axis=0).astype(BF16)
        for d in range(1, pn):
            xg_copy(xy, lax.rem(xy + d, pn)).start()

    row_acc[...] = jnp.zeros_like(row_acc)
    backward_pair(0)

    def early(t):
        backward_pair(t)
        xy_start(t - 1)

    loop(early, 1, min(LATE, pairs))

    def middle(t):
        backward_pair(t)
        back_short_pair(t - LATE)
        xy_start(t - 1)

    loop(middle, LATE, pairs)
    xy_start(pairs - 1)
    loop(back_short_pair, max(pairs - LATE, 0), pairs)
    row2_out[...] = across(row_acc[...])
    row2_copy = remote(row2_out, row2_in, row_send.at[1], row_recv.at[1], pair)
    row2_copy.start()

    quarter = max(pairs // 4, 1)
    loop(forward_pair, 0, quarter)
    z_start()
    loop(forward_pair, quarter, min(2 * quarter, pairs))
    z_sum()
    loop(forward_pair, min(2 * quarter, pairs), min(3 * quarter, pairs))
    grads_start()
    loop(forward_pair, min(3 * quarter, pairs), pairs)
    row2_copy.wait()
    mean2[...] = down((row2_out[...] + row2_in[...]) / dim)

    def ig_copy(c):
        return pltpu.make_async_copy(ig_v.at[c], ig_h.at[:, lanes(c)], out_sem.at[1, c])

    def finish(c):
        inv = both(inv_rms[...])
        normed = act[c].astype(F32) * inv
        ig_v[c] = (inv * (f_ext[c, :rows, :] - normed * both(mean2[...]))).astype(BF16)
        ig_copy(c).start()

    loop(finish)

    def half_copy(i, k):
        half = mr_all.at[i, k]
        return remote(half, half, cg_send.at[i], cg_recv.at[i], other_core)

    def mr_copy(c):
        return pltpu.make_async_copy(
            mr_all.at[c // 2, lax.rem(c, 2), pl.ds(0, BLK), :], mr_h.at[:, lanes(c)], out_sem.at[2, c]
        )

    def spread(c):
        mr_copy(c).start()
        x = mr_all[c // 2, lax.rem(c, 2), BLK:, :].astype(F32)
        x = x[:8] + x[8:]
        seg_ref[:, lanes(c)] = x[:SE]
        gg_ref[:, lanes(c)] = x[SE:]

    def arrived(i):
        @pl.when(i != xy)
        def _():
            xg_copy(i, i).wait_recv()

        half_copy(i, core).start()

    loop(arrived, 0, pairs)
    loop(lambda i: spread(2 * i + core), 0, pairs)

    def across_cores(i):
        half_copy(i, core).wait_send()
        half_copy(i, 1 - core).wait_recv()
        spread(2 * i + 1 - core)

    loop(across_cores, 0, pairs)

    for d in range(1, pn):
        p = lax.rem(xy + d, pn)
        xy_copy(p).wait_send()
        xg_copy(xy, p).wait_send()
    for d in range(1, zn):
        z_copy(lax.rem(z + d, zn)).wait_send()

    def drain(c):
        g_copy(c).wait_send()
        head_copy(c).wait_send()
        out_copy(c).wait()
        ig_copy(c).wait()
        mr_copy(c).wait()

    loop(drain)


def hand_over(*arrays):
    count = len(arrays)

    def body(*refs):
        sems = refs[-1]
        loads, stores = [], []
        for src, dst, via, x in zip(refs, refs[count:], refs[2 * count :], arrays):
            parts = x.shape[0] // 64 or 1
            size = x.shape[0] // parts
            for p in range(parts):
                at, n = pl.ds(p * size, size), len(loads)
                loads.append(pltpu.make_async_copy(src.at[at], via.at[at], sems.at[0, n]))
                stores.append(pltpu.make_async_copy(via.at[at], dst.at[at], sems.at[1, n]))
        for load in loads:
            load.start()
        for load, store in zip(loads, stores):
            load.wait()
            store.start()
        for store in stores:
            store.wait()

    any_spec = pl.BlockSpec(memory_space=pl.ANY)
    return pl.pallas_call(
        body,
        out_shape=[jax.ShapeDtypeStruct(x.shape, x.dtype) for x in arrays],
        in_specs=[any_spec] * count,
        out_specs=[any_spec] * count,
        scratch_shapes=[pltpu.VMEM(x.shape, x.dtype) for x in arrays] + [pltpu.SemaphoreType.DMA((2, 16))],
        compiler_params=pltpu.CompilerParams(vmem_limit_bytes=60 * 1024 * 1024),
        name="hand_over",
    )(*arrays)


def per_device(seq_size, dim, tokens, act, gain, gate, se, mrf, off, cot):
    rows, chans = act.shape
    nc = chans // CH
    zn = 8 if seq_size == 128 else 2
    pn = seq_size // (2 * zn)
    assert nc == 2 * pn and rows == 2 * BLK and mrf.shape[0] == BLK and se.shape[0] == SE
    fwd, inv_hi, inv_lo = transforms()
    any_spec = pl.BlockSpec(memory_space=pl.ANY)
    vmem = pl.BlockSpec(memory_space=pltpu.VMEM)
    smem = pl.BlockSpec(memory_space=pltpu.SMEM)
    part = BLK // zn
    scratch = [
        ((nc, rows, CH), BF16), ((nc, rows, CH), BF16), ((nc, rows, CH), BF16), ((nc, BLK, CH), BF16),
        ((nc, rows, CH), BF16), ((nc, rows, CH), BF16), ((nc, rows, CH), BF16), ((nc, rows, CH), BF16), ((rows, CH), BF16),
        ((nc, rows, CH), BF16), ((nc, rows + 8, CH), F32), ((nc, 8, CH), F32), ((nc, 8, CH), F32),
        ((nc, rows + 8, CH), F32), ((nc, 8, CH), F32), ((nc, rows, CH), F32),
        ((nc, rows, CH), BF16), ((nc, rows, CH), BF16), ((rows, BLK), F32), ((8, rows), F32), ((8, rows), F32),
        ((rows, BLK), F32), ((8, rows), F32), ((8, rows), F32), ((8, CH), F32), ((rows, BLK), F32),
        ((nc, LAGS, CH), F32), ((pn, LAGS, CH), F32), ((pn, LAGS + 8, CH), BF16), ((pn, LAGS + 8, CH), BF16),
        ((LAGS, CH), F32), ((zn, part, CH), F32), ((zn, part, CH), F32), ((8, CH), F32), ((zn, 8, CH), F32), ((LAGS, CH), F32),
        ((pn, 2, LAGS + 8, CH), BF16),
    ]
    sems = [(4, nc), (3, nc), nc, nc, nc, nc, 1, 1, nc, nc, 2, 2, pn, pn, pn, pn, zn, zn, 1, zn, zn, zn, zn, 1, pn, pn, pn, pn]
    sems = [pltpu.SemaphoreType.DMA(s if isinstance(s, tuple) else (s,)) for s in sems]
    out, ig, gg, seg, mr = pl.pallas_call(
        functools.partial(kernel, pn, zn, seq_size, dim, 1.0 / math.sqrt(tokens)),
        out_shape=(
            jax.ShapeDtypeStruct((rows, chans), BF16),
            jax.ShapeDtypeStruct((rows, chans), BF16),
            jax.ShapeDtypeStruct((1, chans), F32),
            jax.ShapeDtypeStruct((SE, chans), F32),
            jax.ShapeDtypeStruct((BLK, chans), BF16),
        ),
        in_specs=[any_spec, vmem, any_spec, vmem, any_spec, smem, any_spec, vmem, vmem, vmem],
        out_specs=(any_spec, any_spec, vmem, vmem, any_spec),
        scratch_shapes=[pltpu.VMEM(*s) for s in scratch] + sems,
        compiler_params=pltpu.CompilerParams(
            collective_id=0, has_side_effects=True, vmem_limit_bytes=58 * 1024 * 1024
        ),
        name="hyena",
    )(act, gain.reshape(1, chans), gate, se, mrf, off, cot, fwd, inv_hi, inv_lo)
    out, ig, gg, seg, mr = hand_over(out, ig, gg, seg, mr)
    return out, ig, gg.reshape(chans), seg, mr


def solution(mesh):
    in_specs = (
        P("seq", "tp"), P("tp"), P("seq", "tp"), P(None, "tp"), P(None, "tp"), P("tp"), P("seq", "tp"),
    )
    out_specs = (P("seq", "tp"), P("seq", "tp"), P("tp"), P(None, "tp"), P(None, "tp"))

    def whole(act, *rest):
        tokens, dim = act.shape
        body = functools.partial(per_device, mesh.shape["seq"], dim, tokens)
        return jax.shard_map(
            body, mesh=mesh, in_specs=in_specs, out_specs=out_specs, check_vma=False
        )(act, *rest)

    return whole
```

time: 120 us -> 81.9 us (0.68)
  Pallas kernels: 113 us -> 81.1 us
  local copies, waits for them, and re-layouts: 6.85 us -> 0 us
    pallas_call x1, Pallas kernels: 113 us -> 76.1 us  [per_device(): pl.pallas_call(functools.partial(kernel, pn, zn, seq_size, dim, 1.0 / mat...]
    unnamed x13 -> x0, local copies, waits for them, and re-layouts: 6.85 us -> none
    pallas_call x0 -> x1, Pallas kernels: none -> 4.98 us  [hand_over(): pl.pallas_call(body, out_shape=[jax.ShapeDtypeStruct(x.shape, x.dtype) fo...]
where the time goes in v2:
time: 81.9 us; the launch traced here: 81.8 us
  Pallas kernels  81.1 us (99%)
    pallas_call x1, Pallas kernels, per_device(): pl.pallas_call(functools.partial(kernel, pn, zn, seq_size, dim, 1.0 / mat...  76.1 us
    pallas_call x1, Pallas kernels, hand_over(): pl.pallas_call(body, out_shape=[jax.ShapeDtypeStruct(x.shape, x.dtype) fo...  4.98 us

profile of v2, /device:TPU:1, one launch (start us, length us, event | category | flops | bytes accessed | tf_op | source)
XLA Modules:
  0.0 81.8 jit_solution(12047308767882316719)
XLA Ops:
  0.6 76.1 %hyena.1 = (bf16[256,4096]{1,0:T(8,128)(2,1)}, bf16[256,4096]{1,0:T(8,128)(2,1)}, f32[1,4096]{1,0:T(1,128)}, f32[7,4096]{1,0:T(8,128)}, bf16[128,4096]{1,0:T(8,128)(2,1)}) custom-call(bf16[256,4096]{1,0:T(8,128)(2,1)} %act_h.1, f32[1,4096]{1,0:T(1,128)} %bitcast.2, bf16[256,4096]{1,0:T(8,128)(2,1)} %gate_h.1, f32[7,4096]{1,0:T(8,128)} %se_ref.1, ...), custom_call_target="tpu_custom_call" | custom-call | tf_op jit(solution)/shard_map/hyena/pallas_call | solution.py:598
  76.8 5.0 %hand_over.1 = (bf16[256,4096]{1,0:T(8,128)(2,1)}, bf16[256,4096]{1,0:T(8,128)(2,1)}, f32[1,4096]{1,0:T(1,128)}, f32[7,4096]{1,0:T(8,128)}, bf16[128,4096]{1,0:T(8,128)(2,1)}) custom-call(bf16[256,4096]{1,0:T(8,128)(2,1)} %get-tuple-element.15.refs_0_, bf16[256,4096]{1,0:T(8,128)(2,1)} %get-tuple-element.16.refs_1_, f32[1,4096]{1,0:T(1,128)} %get-tuple-element.17.refs_2_, ...), custom_call_target="tpu_custom_call" | custom-call | tf_op jit(solution)/shard_map/hand_over/pallas_call | solution.py:563

commit v3 on v2

--- a/solution.py
+++ b/solution.py
@@ -14,7 +14,7 @@
 BLK = 128
 SE = 7
 LAGS = BLK + 8
-LATE = 3
+NEAR = BLK + 16
 F32 = jnp.float32
 BF16 = jnp.bfloat16
 
@@ -54,10 +54,10 @@
     pn, zn, seq_size, dim, scale,
     act_h, gain_ref, gate_h, se_ref, mrf_h, off_ref, cot_h, fwd_ref, inv_hi_ref, inv_lo_ref,
     out_h, ig_h, gg_ref, seg_ref, mr_h,
-    act, gate, cot, mrf, g_own, g_halo, s_own, s_halo, zeros, f_own, f_ext, tail_out, tail_in, b_ext, head_in, spec,
+    act, gate, cot, mrf, g_own, g_halo, f_own, f_halo, zeros, tail, ext, scaled, b_ext, head_in, spec,
     out_v, ig_v, row_acc, row_out, row_in, inv_rms, row2_out, row2_in, no_rows, mean2,
     red, core_in, xy_out, xy_in, own_sum, z_out, z_in, z_last_out, z_last_in, lags, mr_all,
-    in_sem, out_sem, g_send, g_recv, s_send, s_recv, tail_send, tail_recv, head_send, head_recv, row_send, row_recv,
+    in_sem, out_sem, g_send, g_recv, f_send, f_recv, tail_send, tail_recv, head_send, head_recv, row_send, row_recv,
     core_send, core_recv, xy_send, xy_recv, z_send, z_recv, zl_send, zl_recv, zg_send, zg_recv, zgl_send, zgl_recv, xg_send, xg_recv, cg_send, cg_recv,
 ):
     nc = act.shape[0]
@@ -84,6 +84,7 @@
         return lax.rem(start + pn - t, pn)
 
     before_xy = lax.rem(seq + seq_size - 1, seq_size) // (2 * zn)
+    after_xy = lax.rem(seq + 1, seq_size) // (2 * zn)
 
     def lanes(c):
         return pl.ds(pl.multiple_of(c * CH, CH), CH)
@@ -140,28 +141,30 @@
     row_copy = remote(row_out, row_in, row_send.at[0], row_recv.at[0], pair)
     row_copy.start()
 
-    def g_copy(c, src=None):
-        return remote(g_own.at[c] if src is None else src, g_halo.at[c], g_send.at[c], g_recv.at[c], before)
-
-    def gated(c):
-        in_copy(1, c).wait()
-        in_copy(2, c).wait()
-        g_own[c] = (cot[c].astype(F32) * gate[c].astype(F32)).astype(BF16)
-
+    def g_copy(n, c, src=None):
+        at = pl.ds(n * NEAR, rows - NEAR if n else NEAR)
+        src = g_own.at[c, at, :] if src is None else src.at[at, :]
+        return remote(src, g_halo.at[c, at, :], g_send.at[n, c], g_recv.at[n, c], before)
+
+    def g_start(n, c):
         @pl.when(first)
         def _():
-            g_copy(c, zeros).start()
+            g_copy(n, c, zeros).start()
 
         @pl.when(jnp.logical_not(first))
         def _():
-            g_copy(c).start()
+            g_copy(n, c).start()
 
     def gated_pair(t):
         i = turn(before_xy, t)
         for c in (2 * i, 2 * i + 1):
-            gated(c)
+            in_copy(1, c).wait()
+            in_copy(2, c).wait()
+            g_own[c] = (cot[c].astype(F32) * gate[c].astype(F32)).astype(BF16)
+            g_start(0, c)
 
     loop(gated_pair, 0, pairs)
+    loop(lambda c: g_start(1, c))
 
     def filtered(i):
         for n in range(4):
@@ -174,84 +177,54 @@
     row_copy.wait()
     inv_rms[...] = down(lax.rsqrt((row_out[...] + row_in[...]) / dim + 1e-06))
 
-    def feature(c, at):
-        return (act[c, at].astype(F32) * both(inv_rms[at]) * gain_ref[:, lanes(c)]).astype(BF16)
-
-    def tail(c):
-        end = feature(c, slice(rows - 16, rows)).astype(F32)
-        tail_out[c] = jnp.where(last, 0.0, end[8:])
-
-    loop(tail)
-    tail_copy = remote(tail_out, tail_in, tail_send.at[0], tail_recv.at[0], after)
-    tail_copy.start()
-
-    def short_rows(c, r, count):
-        taps = se_ref[:, lanes(c)]
-        total = taps[0:1] * f_ext[c, 8 + r : 8 + r + count, :]
-        for k in range(1, SE):
-            total = total + taps[k : k + 1] * f_ext[c, 8 + r - k : 8 + r + count - k, :]
-        s_own[c, r : r + count, :] = total.astype(BF16)
-
-    def featured(c):
-        f = feature(c, slice(0, rows))
-        f_own[c] = f
-        f_ext[c, 8:, :] = f.astype(F32)
-        short_rows(c, 16, 48)
-        for r in range(64, rows, 64):
-            short_rows(c, r, 64)
-
-    loop(featured)
-    tail_copy.wait()
-
-    def s_copy(c, src=None):
-        return remote(s_own.at[c] if src is None else src, s_halo.at[c], s_send.at[c], s_recv.at[c], after)
-
-    def short(c):
-        f_ext[c, :8, :] = tail_in[c]
-        short_rows(c, 0, 16)
-
+    def f_copy(n, c, src=None):
+        at = pl.ds(n * BLK, BLK)
+        src = f_own.at[c, at, :] if src is None else src.at[at, :]
+        return remote(src, f_halo.at[c, at, :], f_send.at[n, c], f_recv.at[n, c], after)
+
+    def f_start(n, c):
         @pl.when(last)
         def _():
-            s_copy(c, zeros).start()
+            f_copy(n, c, zeros).start()
 
         @pl.when(jnp.logical_not(last))
         def _():
-            s_copy(c).start()
-
-    loop(short)
+            f_copy(n, c).start()
+
+    def featured_pair(t):
+        i = turn(after_xy, t)
+        for c in (2 * i, 2 * i + 1):
+            f_own[c] = (act[c].astype(F32) * both(inv_rms[...]) * gain_ref[:, lanes(c)]).astype(BF16)
+            f_start(1, c)
+
+    loop(featured_pair, 0, pairs)
+    loop(lambda c: f_start(0, c))
 
     def upper(c):
         left = jnp.full((BLK, BLK), off_ref[2 * c], jnp.int32)
         right = jnp.full((BLK, BLK), off_ref[2 * c + 1], jnp.int32)
         return jnp.concatenate([left, right], axis=1).astype(F32)
 
-    def backward(c):
+    def lag_sums(c):
         flag = upper(c)
         up = flag.astype(BF16) > 0.5
-        g0, g1 = g_own[c, :BLK], g_own[c, BLK:]
-        g2, g3 = g_halo[c, :BLK], g_halo[c, BLK:]
-        v0, v1, v2 = jnp.where(up, g1, g0), jnp.where(up, g2, g1), jnp.where(up, g3, g2)
-        hr, hi = spec[c, :BLK], spec[c, BLK:]
+        g0, g1, g2 = g_own[c, :BLK], g_own[c, BLK:], g_halo[c, :BLK]
+        fm, f0, f1 = f_halo[c, BLK:], f_own[c, :BLK], f_own[c, BLK:]
         kr, ki = 0.0, 0.0
-        for n, window in enumerate(((v0, v1), (v1, v2))):
-            at = slice(n * BLK, (n + 1) * BLK)
+        for window, f in (((g0, g1), jnp.where(up, fm, f0)), ((g1, g2), jnp.where(up, f0, f1))):
             v = dot(fwd_ref[...], jnp.concatenate(window, axis=0))
-            vr, vi = v[:BLK], v[BLK:]
-            prod = jnp.concatenate([hr * vr + hi * vi, hr * vi - hi * vr], axis=0).astype(BF16)
-            b_ext[c, at, :] = dot(inv_lo_ref[:BLK, : 2 * BLK], prod)
-            s = dot(fwd_ref[:, :BLK], f_own[c, at])
-            sr, si = s[:BLK], s[BLK:]
+            s = dot(fwd_ref[:, :BLK], f)
+            vr, vi, sr, si = v[:BLK], v[BLK:], s[:BLK], s[BLK:]
             kr = kr + (sr * vr + si * vi)
             ki = ki + (sr * vi - si * vr)
         top, low = split(jnp.concatenate([kr, ki], axis=0))
         x = dot(inv_lo_ref[...], jnp.concatenate([top, low], axis=0))
         red[c, :BLK, :] = x[:BLK]
         up8 = flag[:8] > 0.5
-        f0 = f_own[c, BLK - 16 : BLK].astype(F32)[8:]
-        f1 = f_own[c, rows - 16 : rows].astype(F32)[8:]
-        fa, fb = jnp.where(up8, tail_in[c], f0), jnp.where(up8, f0, f1)
+        em, e0, e1 = (f[BLK - 16 :].astype(F32)[8:] for f in (fm, f0, f1))
+        fa, fb = jnp.where(up8, em, e0), jnp.where(up8, e0, e1)
         ua = g0[:16].astype(F32)[:8] + g2[:16].astype(F32)[:8]
-        ub = g1[:16].astype(F32)[:8] + g3[:16].astype(F32)[:8]
+        ub = g1[:16].astype(F32)[:8] + g_halo[c, BLK:NEAR].astype(F32)[:8]
         row = lax.broadcasted_iota(jnp.int32, (8, CH), 0)
         fix = x[BLK:]
         for r in range(1, SE - 1):
@@ -260,6 +233,18 @@
             fix = fix + jnp.where(row == r, term, 0.0)
         red[c, BLK:, :] = fix
 
+    def backward(c):
+        up = upper(c).astype(BF16) > 0.5
+        g0, g1 = g_own[c, :BLK], g_own[c, BLK:]
+        g2, g3 = g_halo[c, :BLK], g_halo[c, BLK:]
+        v0, v1, v2 = jnp.where(up, g1, g0), jnp.where(up, g2, g1), jnp.where(up, g3, g2)
+        hr, hi = spec[c, :BLK], spec[c, BLK:]
+        for n, window in enumerate(((v0, v1), (v1, v2))):
+            v = dot(fwd_ref[...], jnp.concatenate(window, axis=0))
+            vr, vi = v[:BLK], v[BLK:]
+            prod = jnp.concatenate([hr * vr + hi * vi, hr * vi - hi * vr], axis=0).astype(BF16)
+            b_ext[c, n * BLK : (n + 1) * BLK, :] = dot(inv_lo_ref[:BLK, : 2 * BLK], prod)
+
     def head_copy(c, src=None):
         src = b_ext.at[c, pl.ds(0, 8), :] if src is None else src
         return remote(src, head_in.at[c], head_send.at[c], head_recv.at[c], before)
@@ -267,13 +252,20 @@
     def core_copy(i):
         return remote(red.at[2 * i + 1 - core], core_in.at[i], core_send.at[i], core_recv.at[i], other_core)
 
-    def backward_pair(t):
+    def lag_pair(t):
         i = turn(xy, t)
         for c in (2 * i, 2 * i + 1):
-            g_copy(c).wait_recv()
+            g_copy(0, c).wait_recv()
+            f_copy(1, c).wait_recv()
+        for c in (2 * i, 2 * i + 1):
+            lag_sums(c)
+        core_copy(i).start()
+
+    def backward_pair(i):
+        for c in (2 * i, 2 * i + 1):
+            g_copy(1, c).wait_recv()
         for c in (2 * i, 2 * i + 1):
             backward(c)
-        core_copy(i).start()
         for c in (2 * i, 2 * i + 1):
 
             @pl.when(first)
@@ -293,15 +285,14 @@
             grad = taps[0:1] * b_ext[c, at, :]
             for k in range(1, SE):
                 grad = grad + taps[k : k + 1] * b_ext[c, r + k : r + k + 64, :]
-            scaled = grad * gain
-            inner = scaled * (act[c, at].astype(F32) * both(inv_rms[at]))
+            grad = grad * gain
+            inner = grad * (act[c, at].astype(F32) * both(inv_rms[at]))
             row_acc[at] += inner[:, :BLK] + inner[:, BLK:]
-            f_ext[c, at, :] = scaled
-
-    def back_short_pair(t):
-        i = turn(xy, t)
-        for c in (2 * i, 2 * i + 1):
-            head_copy(c).wait_recv()
+            scaled[c, at, :] = grad
+
+    def back_short_pair(i):
+        for c in (2 * i, 2 * i + 1):
+            head_copy(c).wait()
         for c in (2 * i, 2 * i + 1):
             back_short(c)
 
@@ -327,15 +318,24 @@
     def out_copy(c):
         return pltpu.make_async_copy(out_v.at[c], out_h.at[:, lanes(c)], out_sem.at[0, c])
 
-    def forward(c):
-        up = upper(c).astype(BF16) > 0.5
-        s0, s1 = s_halo[c, :BLK], s_halo[c, BLK:]
-        s2, s3 = s_own[c, :BLK], s_own[c, BLK:]
-        w0, w1, w2 = jnp.where(up, s0, s1), jnp.where(up, s1, s2), jnp.where(up, s2, s3)
+    def forward(c, n):
+        flag = upper(c)
+        up = flag.astype(BF16) > 0.5
+        fl, fm, f0, f1 = f_halo[c, :BLK], f_halo[c, BLK:], f_own[c, :BLK], f_own[c, BLK:]
+        ext[n, :8, :] = jnp.where(flag[:8] > 0.5, tail[c].astype(F32)[8:], fl[BLK - 16 :].astype(F32)[8:])
+        for b, f in enumerate((jnp.where(up, fl, fm), jnp.where(up, fm, f0), jnp.where(up, f0, f1))):
+            ext[n, 8 + b * BLK : 8 + (b + 1) * BLK, :] = f.astype(F32)
+        taps = se_ref[:, lanes(c)]
+        short = []
+        for r in range(8, 8 + 3 * BLK, 64):
+            total = taps[0:1] * ext[n, r : r + 64, :]
+            for k in range(1, SE):
+                total = total + taps[k : k + 1] * ext[n, r - k : r + 64 - k, :]
+            short.append(total.astype(BF16))
         hr, hi = spec[c, :BLK], spec[c, BLK:]
-        for n, window in enumerate(((w0, w1), (w1, w2))):
-            at = slice(n * BLK, (n + 1) * BLK)
-            w = dot(fwd_ref[...], jnp.concatenate(window, axis=0))
+        for b in range(2):
+            at = slice(b * BLK, (b + 1) * BLK)
+            w = dot(fwd_ref[...], jnp.concatenate(short[2 * b : 2 * b + 4], axis=0))
             wr, wi = w[:BLK], w[BLK:]
             prod = jnp.concatenate([hr * wr - hi * wi, hr * wi + hi * wr], axis=0).astype(BF16)
             y = dot(inv_hi_ref[...], prod)
@@ -343,9 +343,9 @@
 
     def forward_pair(i):
         for c in (2 * i, 2 * i + 1):
-            s_copy(c).wait()
-        for c in (2 * i, 2 * i + 1):
-            forward(c)
+            f_copy(0, c).wait_recv()
+        for n in range(2):
+            forward(2 * i + n, n)
         for c in (2 * i, 2 * i + 1):
             out_copy(c).start()
 
@@ -445,35 +445,37 @@
         for d in range(1, pn):
             xg_copy(xy, lax.rem(xy + d, pn)).start()
 
+    def first_lags(t):
+        lag_pair(t)
+
+    def lags_and_sums(t):
+        lag_pair(t)
+        xy_start(t - 1)
+
+    loop(first_lags, 0, 1)
+    loop(lags_and_sums, 1, pairs)
+    tail_copy = remote(
+        f_halo.at[:, pl.ds(rows - 16, 16), :], tail, tail_send.at[0], tail_recv.at[0], after
+    )
+    tail_copy.start()
+    xy_start(pairs - 1)
+
+    half = pairs // 2
     row_acc[...] = jnp.zeros_like(row_acc)
-    backward_pair(0)
-
-    def early(t):
-        backward_pair(t)
-        xy_start(t - 1)
-
-    loop(early, 1, min(LATE, pairs))
-
-    def middle(t):
-        backward_pair(t)
-        back_short_pair(t - LATE)
-        xy_start(t - 1)
-
-    loop(middle, LATE, pairs)
-    xy_start(pairs - 1)
-    loop(back_short_pair, max(pairs - LATE, 0), pairs)
+    loop(backward_pair, 0, pairs)
+    loop(back_short_pair, 0, pairs)
     row2_out[...] = across(row_acc[...])
     row2_copy = remote(row2_out, row2_in, row_send.at[1], row_recv.at[1], pair)
     row2_copy.start()
-
-    quarter = max(pairs // 4, 1)
-    loop(forward_pair, 0, quarter)
+    tail_copy.wait()
+
+    @pl.when(first)
+    def _():
+        tail[...] = jnp.zeros_like(tail)
+
     z_start()
-    loop(forward_pair, quarter, min(2 * quarter, pairs))
+    loop(forward_pair, 0, half)
     z_sum()
-    loop(forward_pair, min(2 * quarter, pairs), min(3 * quarter, pairs))
-    grads_start()
-    loop(forward_pair, min(3 * quarter, pairs), pairs)
     row2_copy.wait()
     mean2[...] = down((row2_out[...] + row2_in[...]) / dim)
 
@@ -483,10 +485,12 @@
     def finish(c):
         inv = both(inv_rms[...])
         normed = act[c].astype(F32) * inv
-        ig_v[c] = (inv * (f_ext[c, :rows, :] - normed * both(mean2[...]))).astype(BF16)
+        ig_v[c] = (inv * (scaled[c] - normed * both(mean2[...]))).astype(BF16)
         ig_copy(c).start()
 
     loop(finish)
+    grads_start()
+    loop(forward_pair, half, pairs)
 
     def half_copy(i, k):
         half = mr_all.at[i, k]
@@ -529,8 +533,9 @@
         z_copy(lax.rem(z + d, zn)).wait_send()
 
     def drain(c):
-        g_copy(c).wait_send()
-        head_copy(c).wait_send()
+        for n in range(2):
+            g_copy(n, c).wait_send()
+            f_copy(n, c).wait_send()
         out_copy(c).wait()
         ig_copy(c).wait()
         mr_copy(c).wait()
@@ -585,15 +590,15 @@
     scratch = [
         ((nc, rows, CH), BF16), ((nc, rows, CH), BF16), ((nc, rows, CH), BF16), ((nc, BLK, CH), BF16),
         ((nc, rows, CH), BF16), ((nc, rows, CH), BF16), ((nc, rows, CH), BF16), ((nc, rows, CH), BF16), ((rows, CH), BF16),
-        ((nc, rows, CH), BF16), ((nc, rows + 8, CH), F32), ((nc, 8, CH), F32), ((nc, 8, CH), F32),
-        ((nc, rows + 8, CH), F32), ((nc, 8, CH), F32), ((nc, rows, CH), F32),
+        ((nc, 16, CH), BF16), ((2, 3 * BLK + 8, CH), F32), ((nc, rows, CH), F32), ((nc, rows + 8, CH), F32),
+        ((nc, 8, CH), F32), ((nc, rows, CH), F32),
         ((nc, rows, CH), BF16), ((nc, rows, CH), BF16), ((rows, BLK), F32), ((8, rows), F32), ((8, rows), F32),
         ((rows, BLK), F32), ((8, rows), F32), ((8, rows), F32), ((8, CH), F32), ((rows, BLK), F32),
         ((nc, LAGS, CH), F32), ((pn, LAGS, CH), F32), ((pn, LAGS + 8, CH), BF16), ((pn, LAGS + 8, CH), BF16),
         ((LAGS, CH), F32), ((zn, part, CH), F32), ((zn, part, CH), F32), ((8, CH), F32), ((zn, 8, CH), F32), ((LAGS, CH), F32),
         ((pn, 2, LAGS + 8, CH), BF16),
     ]
-    sems = [(4, nc), (3, nc), nc, nc, nc, nc, 1, 1, nc, nc, 2, 2, pn, pn, pn, pn, zn, zn, 1, zn, zn, zn, zn, 1, pn, pn, pn, pn]
+    sems = [(4, nc), (3, nc), (2, nc), (2, nc), (2, nc), (2, nc), 1, 1, nc, nc, 2, 2, pn, pn, pn, pn, zn, zn, 1, zn, zn, zn, zn, 1, pn, pn, pn, pn]
     sems = [pltpu.SemaphoreType.DMA(s if isinstance(s, tuple) else (s,)) for s in sems]
     out, ig, gg, seg, mr = pl.pallas_call(
         functools.partial(kernel, pn, zn, seq_size, dim, 1.0 / math.sqrt(tokens)),

time: 81.9 us -> 79.7 us (0.973)
  Pallas kernels: 81.1 us -> 79 us
    pallas_call x1, Pallas kernels: 76.1 us -> 74 us  [per_device(): pl.pallas_call(functools.partial(kernel, pn, zn, seq_size, dim, 1.0 / mat...]
where the time goes in v3:
time: 79.7 us; the launch traced here: 79.6 us
  Pallas kernels  79 us (99%)
    pallas_call x1, Pallas kernels, per_device(): pl.pallas_call(functools.partial(kernel, pn, zn, seq_size, dim, 1.0 / mat...  74 us
    pallas_call x1, Pallas kernels, hand_over(): pl.pallas_call(body, out_shape=[jax.ShapeDtypeStruct(x.shape, x.dtype) fo...  4.98 us

profile of v3, /device:TPU:1, one launch (start us, length us, event | category | flops | bytes accessed | tf_op | source)
XLA Modules:
  0.0 79.6 jit_solution(5083391322867449625)
XLA Ops:
  0.6 74.0 %hyena.1 = (bf16[256,4096]{1,0:T(8,128)(2,1)}, bf16[256,4096]{1,0:T(8,128)(2,1)}, f32[1,4096]{1,0:T(1,128)}, f32[7,4096]{1,0:T(8,128)}, bf16[128,4096]{1,0:T(8,128)(2,1)}) custom-call(bf16[256,4096]{1,0:T(8,128)(2,1)} %act_h.1, f32[1,4096]{1,0:T(1,128)} %bitcast.2, bf16[256,4096]{1,0:T(8,128)(2,1)} %gate_h.1, f32[7,4096]{1,0:T(8,128)} %se_ref.1, ...), custom_call_target="tpu_custom_call" | custom-call | tf_op jit(solution)/shard_map/hyena/pallas_call | solution.py:603
  74.6 5.0 %hand_over.1 = (bf16[256,4096]{1,0:T(8,128)(2,1)}, bf16[256,4096]{1,0:T(8,128)(2,1)}, f32[1,4096]{1,0:T(1,128)}, f32[7,4096]{1,0:T(8,128)}, bf16[128,4096]{1,0:T(8,128)(2,1)}) custom-call(bf16[256,4096]{1,0:T(8,128)(2,1)} %get-tuple-element.15.refs_0_, bf16[256,4096]{1,0:T(8,128)(2,1)} %get-tuple-element.16.refs_1_, f32[1,4096]{1,0:T(1,128)} %get-tuple-element.17.refs_2_, ...), custom_call_target="tpu_custom_call" | custom-call | tf_op jit(solution)/shard_map/hand_over/pallas_call | solution.py:568
